TPU v7x, 128 devices: a whole 4x4x4 slice. The times are simulated.
128 devices in a mesh: grid: 32 (over y, x, core), band: 4 (over z).
Axes of the slice: x: 4, y: 4, z: 4, core: 2. Of those that a mesh axis runs over, the one named last changes fastest.
Arguments:
- residual: float32 [32, 256, 32, 384], P('band', 'grid')
- direction: float32 [32, 256, 32, 384], P('band', 'grid'), may hold values from -2 to 2
- solution: float32 [32, 256, 32, 384], P('band', 'grid'), may hold values from -6 to 6
- old_product: float32 [32], P('band'), may hold values from 629145.6 to 2516582.5
- orbitals: bfloat16 [32, 256, 32, 384], P('band', 'grid')
- energies: float32 [32], replicated, may hold values from -3 to -0.3
- potential: float32 [256, 32, 384], P('grid'), may hold values from 0.5 to 3
- column_index: int32 [32], P('band'), may hold values from 0 to 95
- panel_index: int32 [32], P('band'), may hold values from 0 to 1
Outputs:
- new_solution: float32 [32, 256, 32, 384], P('band', 'grid')
- new_residual: float32 [32, 256, 32, 384], P('band', 'grid')
- new_direction: float32 [32, 256, 32, 384], P('band', 'grid')
- new_product: float32 [32], P('band')
All inputs are finite; a program needn't handle non-finite values.
Results may differ from a plain program's by a relative error of at most 0.00085.
Values may be sent and summed in bfloat16 or wider, within the bound.
A program may use at most 128 MiB of HBM per device.

v0:
```python
import jax
import jax.numpy as jnp
from jax import lax
from jax.sharding import PartitionSpec as P

PB = 16


COEFFS = (-49.0 / 18.0, 3.0 / 2.0, -3.0 / 20.0, 1.0 / 90.0)


def extended(cells, sides, width):
    for axis, dim in sides:
        count = lax.axis_size(axis)
        ends = count - 1
        head = lax.slice_in_dim(cells, 0, width, axis=dim)
        tail = lax.slice_in_dim(cells, cells.shape[dim] - width, cells.shape[dim], axis=dim)
        cells = jnp.concatenate(
            [
                lax.ppermute(tail, axis, [(i, (i + 1) % count) for i in range(ends)]),
                cells,
                lax.ppermute(head, axis, [((i + 1) % count, i) for i in range(ends)]),
            ],
            axis=dim,
        )
    return cells


def stencil(padded, fields, shifted):
    extent_x, extent_y, extent_z = (fields.shape[1], fields.shape[2], fields.shape[3])
    widened = jnp.pad(padded, ((0, 0), (0, 0), (3, 3), (3, 3)))
    summed = 3.0 * COEFFS[0] * fields
    for offset in range(1, 4):
        beside_all = (
            widened[:, 3 + offset : 3 + offset + extent_x, 3 : 3 + extent_y, 3 : 3 + extent_z]
            + widened[:, 3 - offset : 3 - offset + extent_x, 3 : 3 + extent_y, 3 : 3 + extent_z]
        )
        beside_all = (
            beside_all
            + widened[:, 3 : 3 + extent_x, 3 + offset : 3 + offset + extent_y, 3 : 3 + extent_z]
            + widened[:, 3 : 3 + extent_x, 3 - offset : 3 - offset + extent_y, 3 : 3 + extent_z]
        )
        beside_all = (
            beside_all
            + widened[:, 3 : 3 + extent_x, 3 : 3 + extent_y, 3 + offset : 3 + offset + extent_z]
            + widened[:, 3 : 3 + extent_x, 3 : 3 + extent_y, 3 - offset : 3 - offset + extent_z]
        )
        summed = summed + COEFFS[offset] * beside_all
    return -0.5 * summed + shifted * fields


def cell_sum(left, right):
    return jnp.sum(left * right, axis=(1, 2, 3))


def on_device(
    residual,
    direction,
    solution,
    old_product,
    orbitals,
    energies,
    potential,
    column_index,
    panel_index,
):
    band_ids = lax.iota(jnp.int32, energies.shape[0])
    picked = jnp.where(
        band_ids[None, :] == (column_index // 3)[:, None], energies[None, :], jnp.float32(0.0)
    )
    energy = jnp.sum(picked, axis=1)
    shifted = potential[None] - energy[:, None, None, None]
    precond = shifted - 1.5 * COEFFS[0]
    start = residual / precond
    wave = lax.all_gather(orbitals, "band", axis=0, tiled=True)
    cells = float(residual.shape[1] * lax.axis_size("grid") * residual.shape[2] * residual.shape[3])
    member = band_ids[None, :] // PB == panel_index[:, None]
    correlation_local = jnp.einsum(
        "cxyz,bxyz->cb",
        start,
        wave,
        precision=lax.Precision.HIGHEST,
        preferred_element_type=jnp.float32,
    )
    correlation = lax.psum(correlation_local, "grid")
    chosen = jnp.where(member, correlation, jnp.float32(0.0)) / cells
    removed = jnp.einsum(
        "cb,bxyz->cxyz",
        chosen,
        wave,
        precision=lax.Precision.HIGHEST,
        preferred_element_type=jnp.float32,
    )
    projected, chosen = (start - removed, chosen)
    rr_now = lax.psum(cell_sum(residual, projected), "grid")
    new_dir = projected + (rr_now / old_product)[:, None, None, None] * direction
    padded = extended(new_dir.astype(jnp.bfloat16), (("grid", 1),), 3).astype(new_dir.dtype)
    image = stencil(padded, new_dir, shifted)
    curvature = lax.psum(cell_sum(new_dir, image), "grid")
    step_size = (rr_now / curvature)[:, None, None, None]
    return (solution + step_size * new_dir, residual - step_size * image, new_dir, rr_now)


def solution(mesh):
    return jax.shard_map(
        on_device,
        mesh=mesh,
        in_specs=(
            P("band", "grid", None, None),
            P("band", "grid", None, None),
            P("band", "grid", None, None),
            P("band"),
            P("band", "grid", None, None),
            P(),
            P("grid", None, None),
            P("band"),
            P("band"),
        ),
        out_specs=(
            P("band", "grid", None, None),
            P("band", "grid", None, None),
            P("band", "grid", None, None),
            P("band"),
        ),
        check_vma=False,
    )
```

profile of v0, /device:TPU:1, one launch (start us, length us, event | category | flops | bytes accessed | tf_op | source)
XLA Modules:
  0.0 328.9 jit_solution(3798083043351531917)
XLA Ops:
  7.2 0.0 copy-start.2
  7.2 0.0 copy-start.3
  7.2 0.0 copy-start.1
  7.2 0.0 copy-start
  7.2 0.0 all-gather.2.cloned.1.call-start
  7.3 3.6 %copy.14 = bf16[8,8,32,384]{3,0,2,1:T(8,128)(2,1)} copy(bf16[8,8,32,384]{3,2,1,0:T(8,128)(2,1)} %param.13) | data formatting | bytes 3145728 | tf_op args[4]
  10.9 0.0 all-gather.2.cloned.1.call-update
  10.9 0.5 and_select_fusion
  11.4 0.0 copy-done.2
  11.4 0.0 copy-done.3
  11.4 0.2 select_reduce_fusion
  11.6 68.5 %all-gather.2.cloned.1.call-done = bf16[32,8,32,384]{3,0,2,1:T(8,128)(2,1)} async-done(((bf16[8,8,32,384]{3,0,2,1:T(8,128)(2,1)}), bf16[32,8,32,384]{3,0,2,1:T(8,128)(2,1)}) %all-gather.2.cloned.1.call-update) | async-done | bytes 6291472 | tf_op jit(solution)/shard_map/all_gather | solution.py:75
  80.1 0.0 copy-done.1
  80.2 8.1 %convolution_bitcast_fusion = f32[8,32]{1,0:T(8,128)S(1)} fusion(bf16[32,8,32,384]{3,0,2,1:T(8,128)(2,1)} %all-gather.2.cloned.1.call-done, f32[8,8,32,384]{3,2,1,0:T(8,128)S(1)} %copy-done, f32[8]{0:T(128)S(1)} %select_reduce_fusion, f32[8,32,384]{2,1,0:T(8,128)S(1)} %copy-done.1), kind=kOutput, calls=%fused_computation.46 | convolution fusion | flops 304349184 | bytes 9831456 | tf_op jit(solution)/shard_map/cxyz,bxyz->cb/dot_general | solution.py:78
  88.3 62.7 %psum.21 = f32[8,32]{1,0:T(8,128)S(1)} all-reduce(f32[8,32]{1,0:T(8,128)S(1)} %convolution_bitcast_fusion), channel_id=1, replica_groups=mesh['grid'=32,'band'=4] {'grid'}, use_global_device_ids=true, to_apply=%region_1.2 | all-reduce | flops 256 | bytes 2048 | tf_op jit(solution)/shard_map/psum | solution.py:85
  151.0 0.0 copy-done.4
  151.0 7.8 %multiply_reduce_fusion.1 = (f32[8]{0:T(128)}, f32[8,8,32,384]{3,0,2,1:T(8,128)}) fusion(f32[8,8,32,384]{3,2,1,0:T(8,128)S(1)} %copy-done, bf16[32,8,32,384]{3,0,2,1:T(8,128)(2,1)} %all-gather.2.cloned.1.call-done, f32[8,32]{1,0:T(8,128)S(1)} %psum.21, s32[32]{0:T(128)} %and_select_fusion, s32[8]{0:T(128)S(1)} %copy-done.4, f32[8]{0:T(128)S(1)} %select_reduce_fusion, ...), kind=kOutput, calls=%fused_computation.43 | convolution fusion | flops 306709248 | bytes 12977376 | tf_op jit(solution)/shard_map/cb,bxyz->cxyz/dot_general | solution.py:87
  158.8 67.0 %psum.22 = f32[8]{0:T(128)S(1)} all-reduce(f32[8]{0:T(128)} %get-tuple-element.16), channel_id=1, replica_groups=mesh['grid'=32,'band'=4] {'grid'}, use_global_device_ids=true, to_apply=%region_3.4 | all-reduce | flops 8 | bytes 64 | tf_op jit(solution)/shard_map/psum | solution.py:95
  225.8 0.0 copy-done.5
  225.9 5.1 %fusion.34 = (bf16[8,8,32,384]{3,0,2,1:T(8,128)(2,1)S(1)}, f32[8,8,32,384]{3,0,2,1:T(8,128)S(1)}) fusion(f32[8,8,32,384]{3,0,2,1:T(8,128)} %get-tuple-element.17, f32[8,8,32,384]{3,2,1,0:T(8,128)} %param.10, f32[8]{0:T(128)S(1)} %div.35), kind=kLoop, calls=%fused_computation.64 | loop fusion | flops 2359296 | bytes 11010080 | tf_op jit(solution)/shard_map/convert_element_type | solution.py:97
  231.0 0.1 fusion.36
  231.1 1.9 collective-permute-start
  233.0 2.4 collective-permute-start.1
  235.5 2.2 copy.21
  237.7 2.1 collective-permute-done
  239.8 4.4 %collective-permute-done.1 = bf16[8,3,32,384]{3,0,2,1:T(8,128)(2,1)S(1)} collective-permute-done((bf16[8,3,32,384]{3,0,2,1:T(8,128)(2,1)S(1)}, bf16[8,3,32,384]{3,0,2,1:T(8,128)(2,1)S(1)}, u32[]{:S(2)}, u32[]{:S(2)}) %collective-permute-start.1) | collective-permute-done | bytes 589856 | tf_op jit(solution)/shard_map/ppermute | solution.py:22
  244.2 0.4 maximum_convert_fusion
  244.6 6.7 %multiply_reduce_fusion = (f32[8]{0:T(128)S(1)}, f32[8,8,32,384]{3,0,2,1:T(8,128)}) fusion(f32[8,8,32,384]{3,0,2,1:T(8,128)S(1)} %get-tuple-element.11, f32[8]{0:T(128)S(1)} %select_reduce_fusion, f32[8,32,384]{2,1,0:T(8,128)S(1)} %copy-done.1, f32[8,14,32,384]{3,0,2,1:T(8,128)S(1)} %maximum_convert_fusion), kind=kLoop, calls=%fused_computation.42 | loop fusion | flops 22020088 | bytes 31064608 | tf_op jit(solution)/shard_map/reduce_sum | solution.py:53
  251.4 57.1 %psum.23 = f32[8]{0:T(128)S(1)} all-reduce(f32[8]{0:T(128)S(1)} %get-tuple-element.8), channel_id=1, replica_groups=mesh['grid'=32,'band'=4] {'grid'}, use_global_device_ids=true, to_apply=%region_5.6 | all-reduce | flops 8 | bytes 64 | tf_op jit(solution)/shard_map/psum | solution.py:99
  308.5 9.1 %multiply_subtract_fusion = (f32[8,8,32,384]{3,0,2,1:T(8,128)S(1)}, f32[8,8,32,384]{3,0,2,1:T(8,128)S(1)}) fusion(f32[8,8,32,384]{3,0,2,1:T(8,128)} %get-tuple-element.9, f32[8,8,32,384]{3,2,1,0:T(8,128)} %param.9, f32[8]{0:T(128)S(1)} %div.36, f32[8,8,32,384]{3,0,2,1:T(8,128)S(1)} %get-tuple-element.11, f32[8,8,32,384]{3,2,1,0:T(8,128)} %param.11), kind=kLoop, calls=%fused_computation.41 | loop fusion | flops 3145728 | bytes 18874400 | tf_op jit(solution)/shard_map/sub | solution.py:101
  317.6 2.2 copy.20
  319.8 2.2 copy.19
  (8 shorter events, 0.0 us)
Async XLA Ops:
  7.2 4.2 %copy-start.2 = (s32[8]{0:T(128)S(1)}, s32[8]{0:T(128)}, u32[]{:S(2)}) copy-start(s32[8]{0:T(128)} %param.16) | copy-start | bytes 100
  7.2 4.3 %copy-start.3 = (f32[32]{0:T(128)S(1)}, f32[32]{0:T(128)}, u32[]{:S(2)}) copy-start(f32[32]{0:T(128)} %param.14) | copy-start | bytes 388
  7.2 73.0 %copy-start.1 = (f32[8,32,384]{2,1,0:T(8,128)S(1)}, f32[8,32,384]{2,1,0:T(8,128)}, u32[]{:S(2)}) copy-start(f32[8,32,384]{2,1,0:T(8,128)} %param.15) | copy-start | bytes 1179652
  7.2 73.0 %copy-start = (f32[8,8,32,384]{3,2,1,0:T(8,128)S(1)}, f32[8,8,32,384]{3,2,1,0:T(8,128)}, u32[]{:S(2)}) copy-start(f32[8,8,32,384]{3,2,1,0:T(8,128)} %param.9) | copy-start | bytes 9437188
  7.2 72.9 %all-gather.2.cloned.1.call-start = ((), (), s32[]{:S(2)}) async-start(), calls=%async_computation | async-start | bytes 7864320 | tf_op jit(solution)/shard_map/all_gather | solution.py:75
  11.6 139.4 %copy-start.4 = (s32[8]{0:T(128)S(1)}, s32[8]{0:T(128)}, u32[]{:S(2)}) copy-start(s32[8]{0:T(128)} %param.17) | copy-start | bytes 100
  151.0 74.8 %copy-start.5 = (f32[8]{0:T(128)S(1)}, f32[8]{0:T(128)}, u32[]{:S(2)}) copy-start(f32[8]{0:T(128)} %param.12) | copy-start | bytes 100
  225.8 82.7 %copy-start.6 = (f32[8]{0:T(128)}, f32[8]{0:T(128)S(1)}, u32[]{:S(2)}) copy-start(f32[8]{0:T(128)S(1)} %psum.22) | copy-start | bytes 100
  231.1 8.7 %collective-permute-start = (bf16[8,3,32,384]{3,0,2,1:T(8,128)(2,1)S(1)}, bf16[8,3,32,384]{3,0,2,1:T(8,128)(2,1)S(1)}, u32[]{:S(2)}, u32[]{:S(2)}) collective-permute-start(bf16[8,3,32,384]{3,0,2,1:T(8,128)(2,1)S(1)} %get-tuple-element.12), channel_id=1, source_target_pairs={{0,4},{4,8},{8,12},{12,16},{16,20},{20,24},{24,28},{28,32},{32,36}... | collective-permute-start | bytes 1769480 | tf_op jit(solution)/shard_map/ppermute | solution.py:20
  233.0 11.2 %collective-permute-start.1 = (bf16[8,3,32,384]{3,0,2,1:T(8,128)(2,1)S(1)}, bf16[8,3,32,384]{3,0,2,1:T(8,128)(2,1)S(1)}, u32[]{:S(2)}, u32[]{:S(2)}) collective-permute-start(bf16[8,3,32,384]{3,0,2,1:T(8,128)(2,1)S(1)} %get-tuple-element.13), channel_id=1, source_target_pairs={{4,0},{8,4},{12,8},{16,12},{20,16},{24,20},{28,24},{32,28},{36,32}... | collective-permute-start | bytes 1769480 | tf_op jit(solution)/shard_map/ppermute | solution.py:22
Sparse Core Ops, SparseCore 0:
  11.0 69.0 all-gather.1
where the time goes:
time: 334 us; the launch traced here: 329 us
  blocking collectives  187 us (56%)
  waiting for transfers between devices  75.1 us (22%)
  other arithmetic  22.1 us (7%)
  matrix products  15.9 us (5%)
  between operations  14.1 us (4%)
  local copies, waits for them, and re-layouts  10.5 us (3%)
  starting transfers between devices  4.4 us (1%)
    all_gather x1, waiting for transfers between devices, on_device(): wave = lax.all_gather(orbitals, 'band', axis=0, tiled=True)  68.5 us
    psum x1, blocking collectives, on_device(): rr_now = lax.psum(cell_sum(residual, projected), 'grid')  67 us
    psum x1, blocking collectives, on_device(): correlation = lax.psum(correlation_local, 'grid')  62.7 us
    psum x1, blocking collectives, on_device(): curvature = lax.psum(cell_sum(new_dir, image), 'grid')  57.1 us
    unnamed x18, local copies, waits for them, and re-layouts  10.3 us
    sub x1, other arithmetic, on_device(): residual - step_size * image  9.1 us
    dot_general x1, matrix products, on_device(): jnp.einsum('cxyz,bxyz->cb', start, wave, precision=lax.Precision.HIGHEST,...  8.12 us
    dot_general x1, matrix products, on_device(): jnp.einsum('cb,bxyz->cxyz', chosen, wave, precision=lax.Precision.HIGHEST...  7.77 us
  transfers between devices with their start and end apart: 3, of which 3 were waited for; matrix products, arithmetic and copies ran while one was open for 1% of the time, Pallas kernels for 0%

commit v1 on v0

v1 whole, which is shorter than its diff:
```python
import functools

import jax
import jax.numpy as jnp
from jax import lax
from jax.experimental import pallas as pl
from jax.experimental.pallas import tpu as pltpu
from jax.sharding import PartitionSpec as P

MESH = pl.DeviceIdType.MESH
F32 = jnp.float32
BF16 = jnp.bfloat16

PB = 16
K0, K1, K2, K3 = (-49.0 / 18.0, 3.0 / 2.0, -3.0 / 20.0, 1.0 / 90.0)
SCALED = (135.0, -13.5, 1.0)
UNSCALE = -0.5 / 90.0

COLS = 8
BANDS = 8
XS = 8
NY = 32
NZ = 384
HALF = 16
HALO = 3
CHUNKS = 4


def iota(shape, dim):
    return lax.broadcasted_iota(jnp.int32, shape, dim)


def coefficient(distance):
    gap = jnp.abs(distance)
    return jnp.where(
        gap == 1, SCALED[0], jnp.where(gap == 2, SCALED[1], jnp.where(gap == 3, SCALED[2], 0.0))
    )


def dot(left, right, dims=((1,), (0,)), precision=None):
    return lax.dot_general(
        left, right, (dims, ((), ())), precision=precision, preferred_element_type=F32
    )


def first_kernel(
    groups,
    res_hbm,
    dir_hbm,
    orb_hbm,
    pot_hbm,
    old_ref,
    energy_ref,
    column_ref,
    panel_ref,
    new_dir,
    image,
    rr_out,
    step_out,
    start,
    direction,
    pot,
    wave,
    left,
    acc,
    kron,
    sten,
    sten_halo,
    sten_z,
    halo_out,
    halo_in,
    sums,
    curves,
    partial,
    local_sem,
    ring_send,
    ring_recv,
    sum_send,
    sum_recv,
    halo_send,
    halo_recv,
):
    g = lax.axis_index("grid")
    z = lax.axis_index("band")
    up, down = lax.rem(z + 1, 4), lax.rem(z + 3, 4)

    loads = [
        pltpu.make_async_copy(src, dst, local_sem.at[i])
        for i, (src, dst) in enumerate(
            ((res_hbm, start), (pot_hbm, pot), (orb_hbm, wave.at[0]), (dir_hbm, direction))
        )
    ]
    for load in loads:
        load.start()

    barrier = pltpu.get_barrier_semaphore()
    for to in (up, down):
        pl.semaphore_signal(barrier, inc=1, device_id=(g, to), device_id_type=MESH)

    def greet(k, _):
        pl.semaphore_signal(
            barrier, inc=1, device_id=(lax.rem(g + k, groups), z), device_id_type=MESH
        )
        return 0

    lax.fori_loop(1, groups, greet, 0)
    pl.semaphore_wait(barrier, groups + 1)

    def ring(src, dst, i, to):
        return pltpu.make_async_remote_copy(
            src_ref=src,
            dst_ref=dst,
            send_sem=ring_send.at[i],
            recv_sem=ring_recv.at[i],
            device_id=(g, to),
            device_id_type=MESH,
        )

    low, high = pl.ds(0, BANDS // 2), pl.ds(BANDS // 2, BANDS // 2)
    low_up = ring(orb_hbm.at[low], wave.at[1, low], 0, up)
    high_down = ring(orb_hbm.at[high], wave.at[3, high], 1, down)
    high_up = ring(orb_hbm.at[high], wave.at[1, high], 2, up)
    low_down = ring(orb_hbm.at[low], wave.at[3, low], 3, down)
    low_up.start()
    high_down.start()
    high_up.start()
    low_down.start()

    rows, cols = iota((256, 256), 0), iota((256, 256), 1)
    dx, dy = rows // NY - cols // NY, rows % NY - cols % NY
    sten[...] = jnp.where(
        dy == 0, coefficient(dx), jnp.where(dx == 0, coefficient(dy), 0.0)
    ).astype(BF16)
    rows, cols = iota((256, 192), 0), iota((256, 192), 1)
    plane = cols // NY
    there = jnp.where(plane < HALO, plane - HALO, plane - HALO + XS)
    inside = jnp.where(plane < HALO, g, groups - 1 - g) > 0
    sten_halo[...] = jnp.where(
        jnp.logical_and(inside, rows % NY == cols % NY), coefficient(rows // NY - there), 0.0
    ).astype(BF16)
    sten_z[...] = coefficient(iota((NZ, NZ), 0) - iota((NZ, NZ), 1)).astype(BF16)

    def shift_of(c):
        return energy_ref[column_ref[c] // 3]

    loads[0].wait()
    loads[1].wait()

    def start_column(c, _):
        e = shift_of(c)

        def start_plane(x, total):
            r = start[c, x]
            s = r / (pot[x] - e - 1.5 * K0)
            start[c, x] = s
            for h in range(2):
                part = slice(h * HALF, (h + 1) * HALF)
                left[x, h, 0, c] = s[part].astype(BF16)
                left[x, h, 1, c] = r[part].astype(BF16)
            return total + jnp.sum((r * s).reshape(4, 8, NZ), axis=0)

        total = lax.fori_loop(0, XS, start_plane, jnp.zeros((8, NZ), F32))
        partial[c] = total[:, :128] + total[:, 128:256] + total[:, 256:]
        return 0

    lax.fori_loop(0, COLS, start_column, 0)

    def correlate(slot, first, planes):
        def body(x, total):
            for h in range(2):
                total = total + dot(
                    left[x, h].reshape(256, NZ),
                    wave[slot, :, x, pl.ds(h * HALF, HALF), :].reshape(128, NZ),
                    ((1,), (1,)),
                )
            return total

        return lax.fori_loop(first, first + planes, body, jnp.zeros((256, 128), F32))

    loads[2].wait()
    acc[:, 0:128] = correlate(0, 0, XS)

    forwards = []
    low_up.wait_recv()
    for q in range(CHUNKS):
        part = pl.ds(q * XS // CHUNKS, XS // CHUNKS)
        copy = ring(wave.at[1, low, part], wave.at[2, low, part], 4 + 2 * q, up)
        copy.start()
        forwards.append(copy)
    high_down.wait_recv()
    for q in range(CHUNKS):
        part = pl.ds(q * XS // CHUNKS, XS // CHUNKS)
        copy = ring(wave.at[3, high, part], wave.at[2, high, part], 5 + 2 * q, down)
        copy.start()
        forwards.append(copy)
    high_up.wait_recv()
    acc[:, 128:256] = correlate(1, 0, XS)
    low_down.wait_recv()
    acc[:, 384:512] = correlate(3, 0, XS)
    for q in range(CHUNKS):
        forwards[q].wait_recv()
        forwards[CHUNKS + q].wait_recv()
        part = correlate(2, q * XS // CHUNKS, XS // CHUNKS)
        acc[:, 256:384] = part if q == 0 else acc[:, 256:384] + part

    same = iota((256, 512), 0) % HALF == iota((256, 512), 1) % HALF
    folded = jnp.sum(jnp.where(same, acc[...], 0.0).reshape(16, HALF, 512), axis=1)
    pick = iota((512, 128), 0) // HALF
    lane = iota((512, 128), 1)
    mine = dot(
        folded[:8], jnp.where(pick == lane, 1.0, 0.0), precision=lax.Precision.HIGHEST
    ) + dot(
        folded[8:], jnp.where(pick + 32 == lane, 1.0, 0.0), precision=lax.Precision.HIGHEST
    )
    lane = iota((8, 128), 1)
    own = jnp.sum(jnp.sum(partial[...], axis=1), axis=1, keepdims=True)
    mine = mine + jnp.where(lane == 64, own, 0.0)

    def add_over_grid(table, value, k):
        table[g] = value

        def send(i, _):
            pltpu.make_async_remote_copy(
                src_ref=table.at[g],
                dst_ref=table.at[g],
                send_sem=sum_send.at[k],
                recv_sem=sum_recv.at[k],
                device_id=(lax.rem(g + i, groups), z),
                device_id_type=MESH,
            ).start()
            return 0

        lax.fori_loop(1, groups, send, 0)
        others = table.at[pl.ds(0, groups - 1)]
        pltpu.make_async_copy(others, others, sum_recv.at[k]).wait()
        total = jnp.sum(table[...], axis=0)
        pltpu.make_async_copy(others, others, sum_send.at[k]).wait()
        return total

    total = add_over_grid(sums, mine, 0)

    owner = lax.rem(z + jnp.where(lane < 8, 0, jnp.where(lane < 16, 3, jnp.where(lane < 24, 2, 1))), 4)
    column = iota((8, 128), 0)
    panel = jnp.zeros((8, 128), jnp.int32)
    old = jnp.zeros((8, 128), F32)
    for c in range(COLS):
        panel = jnp.where(column == c, panel_ref[c], panel)
        old = jnp.where(column == c, old_ref[c], old)
    cells = float(groups * XS * NY * NZ)
    chosen = jnp.where(
        jnp.logical_and(lane < 32, owner * BANDS // PB == panel), total, 0.0
    ) / cells
    overlap = pltpu.roll(total, 96, 1)
    rr = jnp.sum(
        jnp.where(lane == 64, total, 0.0) - chosen * overlap, axis=1, keepdims=True
    )
    rr = jnp.broadcast_to(rr, (8, 128))
    rr_out[...] = rr
    beta = rr / old

    top = chosen.astype(BF16)
    rest = (chosen - top.astype(F32)).astype(BF16)
    pair = jnp.concatenate([top.astype(F32), rest.astype(F32)], axis=0).astype(BF16)
    spread = dot(
        jnp.where(iota((256, 16), 0) // HALF == iota((256, 16), 1), 1.0, 0.0).astype(BF16), pair
    ).astype(BF16)
    spread = dot(
        spread,
        jnp.where(iota((128, 512), 1) // HALF == iota((128, 512), 0), 1.0, 0.0).astype(BF16),
    )
    kron[...] = jnp.where(same, spread, 0.0).astype(BF16)

    loads[3].wait()

    def project(x, face, k):
        for h in range(2):
            part = pl.ds(h * HALF, HALF)
            removed = dot(kron[...], wave[:, :, x, part, :].reshape(512, NZ))
            for c in range(COLS):
                gone = removed[c * HALF : (c + 1) * HALF] + removed[128 + c * HALF : 128 + (c + 1) * HALF]
                value = start[c, x, part] - gone + beta[c : c + 1, :1] * direction[c, x, part]
                new_dir[c, x, part] = value
                if face is not None:
                    halo_out[face, c, k, part] = value.astype(BF16)

    def halo(face, to):
        return pltpu.make_async_remote_copy(
            src_ref=halo_out.at[face],
            dst_ref=halo_in.at[1 - face],
            send_sem=halo_send.at[face],
            recv_sem=halo_recv.at[face],
            device_id=(to, z),
            device_id_type=MESH,
        )

    to_left = halo(0, lax.rem(g + groups - 1, groups))
    to_right = halo(1, lax.rem(g + 1, groups))

    def face_plane(face, x, k):
        project(x, face, k)
        return 0

    lax.fori_loop(0, HALO, lambda k, _: face_plane(0, k, k), 0)
    to_left.start()
    lax.fori_loop(0, HALO, lambda k, _: face_plane(1, XS - HALO + k, k), 0)
    to_right.start()
    lax.fori_loop(HALO, XS - HALO, lambda x, _: face_plane(None, x, None), 0)

    def inner(c, _):
        value = new_dir[c].reshape(256, NZ)
        top = value.astype(BF16)
        rest = (value - top.astype(F32)).astype(BF16)
        beside = dot(sten[...], top) + dot(sten[...], rest)
        beside = beside + (dot(top, sten_z[...]) + dot(rest, sten_z[...]))
        local = pot[...].reshape(256, NZ) - shift_of(c) - 1.5 * K0
        image[c] = (UNSCALE * beside + local * value).reshape(XS, NY, NZ)
        return 0

    lax.fori_loop(0, COLS, inner, 0)
    to_left.wait_recv()
    to_right.wait_recv()

    def outer(c, _):
        beside = dot(sten_halo[:, 0:96], halo_in[0, c].reshape(96, NZ)) + dot(
            sten_halo[:, 96:192], halo_in[1, c].reshape(96, NZ)
        )
        full = image[c].reshape(256, NZ) + UNSCALE * beside
        image[c] = full.reshape(XS, NY, NZ)
        total = jnp.sum((full * new_dir[c].reshape(256, NZ)).reshape(32, 8, NZ), axis=0)
        partial[c] = total[:, :128] + total[:, 128:256] + total[:, 256:]
        return 0

    lax.fori_loop(0, COLS, outer, 0)
    curvature = jnp.sum(add_over_grid(curves, jnp.sum(partial[...], axis=1), 1), axis=1, keepdims=True)
    step_out[...] = rr / curvature

    to_left.wait_send()
    to_right.wait_send()
    for copy in (low_up, high_down, high_up, low_down, *forwards):
        copy.wait_send()


def last_kernel(step, solution_in, residual_in, new_dir, image, solution_out, residual_out, dir_out):
    c = pl.program_id(0)
    alpha = step[pl.ds(c, 1), :1]
    p = new_dir[0]
    solution_out[0] = solution_in[0] + alpha * p
    residual_out[0] = residual_in[0] - alpha * image[0]
    dir_out[0] = p


def on_device(groups, residual, direction, solution, old_product, orbitals, energies, potential, column_index, panel_index):
    field = (COLS, XS, NY, NZ)
    any_spec = pl.BlockSpec(memory_space=pl.ANY)
    smem = pl.BlockSpec(memory_space=pltpu.SMEM)
    vmem = pl.BlockSpec(memory_space=pltpu.VMEM)
    dma = pltpu.SemaphoreType.DMA
    new_dir, image, rr, step = pl.pallas_call(
        functools.partial(first_kernel, groups),
        out_shape=(
            jax.ShapeDtypeStruct(field, F32),
            jax.ShapeDtypeStruct(field, F32),
            jax.ShapeDtypeStruct((8, 128), F32),
            jax.ShapeDtypeStruct((8, 128), F32),
        ),
        in_specs=[any_spec] * 4 + [smem] * 4,
        out_specs=(vmem, vmem, vmem, vmem),
        scratch_shapes=[
            pltpu.VMEM(field, F32),
            pltpu.VMEM(field, F32),
            pltpu.VMEM((XS, NY, NZ), F32),
            pltpu.VMEM((4, BANDS, XS, NY, NZ), BF16),
            pltpu.VMEM((XS, 2, 2, COLS, HALF, NZ), BF16),
            pltpu.VMEM((256, 512), F32),
            pltpu.VMEM((256, 512), BF16),
            pltpu.VMEM((256, 256), BF16),
            pltpu.VMEM((256, 192), BF16),
            pltpu.VMEM((NZ, NZ), BF16),
            pltpu.VMEM((2, COLS, HALO, NY, NZ), BF16),
            pltpu.VMEM((2, COLS, HALO, NY, NZ), BF16),
            pltpu.VMEM((groups, 8, 128), F32),
            pltpu.VMEM((groups, 8, 128), F32),
            pltpu.VMEM((COLS, 8, 128), F32),
            dma((4,)),
            dma((4 + 2 * CHUNKS,)),
            dma((4 + 2 * CHUNKS,)),
            dma((2,)),
            dma((2,)),
            dma((2,)),
            dma((2,)),
        ],
        compiler_params=pltpu.CompilerParams(
            collective_id=0, has_side_effects=True, vmem_limit_bytes=40 << 20
        ),
        name="project_and_apply",
    )(residual, direction, orbitals, potential, old_product, energies, column_index, panel_index)

    block = pl.BlockSpec((1, XS, NY, NZ), lambda c: (c, 0, 0, 0))
    new_solution, new_residual, out_dir = pl.pallas_call(
        last_kernel,
        grid=(COLS,),
        out_shape=tuple(jax.ShapeDtypeStruct(field, F32) for _ in range(3)),
        in_specs=[pl.BlockSpec((8, 128), lambda c: (0, 0)), block, block, block, block],
        out_specs=(block, block, block),
        compiler_params=pltpu.CompilerParams(vmem_limit_bytes=16 << 20),
        name="take_step",
    )(step, solution, residual, new_dir, image)
    return new_solution, new_residual, out_dir, rr[:, 0]


def solution(mesh):
    field = P("band", "grid", None, None)
    return jax.shard_map(
        functools.partial(on_device, mesh.shape["grid"]),
        mesh=mesh,
        in_specs=(
            field,
            field,
            field,
            P("band"),
            field,
            P(),
            P("grid", None, None),
            P("band"),
            P("band"),
        ),
        out_specs=(field, field, field, P("band")),
        check_vma=False,
    )
```

time: 334 us -> 104 us (0.31); the launches traced: 329 us -> 104 us
  blocking collectives: 187 us -> 0 us
  Pallas kernels: 0 us -> 93.5 us
  waiting for transfers between devices: 75.1 us -> 0 us
  other arithmetic: 22.1 us -> 0 us
  matrix products: 15.9 us -> 0 us
  between operations: 14.1 us -> 0.66 us
  starting transfers between devices: 4.4 us -> 0 us
    psum x3 -> x0, blocking collectives: 187 us -> none  [the longest x1 67 us: on_device(): rr_now = lax.psum(cell_sum(residual, projected), 'grid')]
    pallas_call x0 -> x2, Pallas kernels: none -> 93.5 us  [the longest x1 88.6 us: on_device(): pl.pallas_call(functools.partial(first_kernel, groups), out_shape=(jax.Sh...]
    all_gather x1 -> x0, waiting for transfers between devices: 68.5 us -> none  [on_device(): wave = lax.all_gather(orbitals, 'band', axis=0, tiled=True)]
    dot_general x2 -> x0, matrix products: 15.9 us -> none  [the longest x1 8.12 us: on_device(): jnp.einsum('cxyz,bxyz->cb', start, wave, precision=lax.Precision.HIGHEST,...]
    sub x1 -> x0, other arithmetic: 9.1 us -> none  [on_device(): residual - step_size * image]
    reduce_sum x2 -> x0, other arithmetic: 6.93 us -> none  [the longest x1 6.75 us: cell_sum(): return jnp.sum(left * right, axis=(1, 2, 3))]
    ppermute x2 -> x0, waiting for transfers between devices: 6.52 us -> none  [the longest x1 4.4 us: extended(): lax.ppermute(head, axis, [((i + 1) % count, i) for i in range(ends)])]
    convert_element_type x2 -> x0, other arithmetic: 5.5 us -> none  [the longest x1 5.09 us: on_device(): new_dir.astype(jnp.bfloat16)]
  transfers between devices with their start and end apart: 3 -> 0, of which waited for: 3 -> 0; matrix products, arithmetic and copies ran while one was open for 1% -> 0% of each run, Pallas kernels for 0% -> 0%
where the time goes in v1:
time: 104 us
  Pallas kernels  93.5 us (90%)
  local copies, waits for them, and re-layouts  9.42 us (9%)
    pallas_call x1, Pallas kernels, on_device(): pl.pallas_call(functools.partial(first_kernel, groups), out_shape=(jax.Sh...  88.6 us
    unnamed x18, local copies, waits for them, and re-layouts  8.8 us
    pallas_call x1, Pallas kernels, on_device(): pl.pallas_call(last_kernel, grid=(COLS,), out_shape=tuple((jax.ShapeDtype...  4.88 us

profile of v1, /device:TPU:1, one launch (start us, length us, event | category | flops | bytes accessed | tf_op | source)
XLA Modules:
  0.0 103.6 jit_solution(16800966094303591837)
XLA Ops:
  0.6 0.0 copy-start
  0.6 1.9 %copy-done = f32[8,8,32,384]{3,2,1,0:T(8,128)S(1)} copy-done((f32[8,8,32,384]{3,2,1,0:T(8,128)S(1)}, f32[8,8,32,384]{3,2,1,0:T(8,128)}, u32[]{:S(2)}) %copy-start) | copy-done | bytes 3145752
  2.5 0.0 copy-start.1
  2.5 1.9 %copy-done.1 = f32[8,8,32,384]{3,2,1,0:T(8,128)S(1)} copy-done((f32[8,8,32,384]{3,2,1,0:T(8,128)S(1)}, f32[8,8,32,384]{3,2,1,0:T(8,128)}, u32[]{:S(2)}) %copy-start.1) | copy-done | bytes 3145752
  4.4 0.0 copy-start.3
  4.4 1.4 %copy-done.3 = bf16[8,8,32,384]{3,2,1,0:T(8,128)(2,1)S(1)} copy-done((bf16[8,8,32,384]{3,2,1,0:T(8,128)(2,1)S(1)}, bf16[8,8,32,384]{3,2,1,0:T(8,128)(2,1)}, u32[]{:S(2)}) %copy-start.3) | copy-done | bytes 1572888
  5.8 0.0 copy-start.4
  5.8 1.0 copy-done.4
  6.8 0.0 copy-start.5
  6.8 0.7 copy-done.5
  7.5 0.0 copy-start.6
  7.5 0.7 copy-done.6
  8.1 0.0 copy-start.7
  8.1 0.7 copy-done.7
  8.8 0.0 copy-start.8
  8.8 0.7 copy-done.8
  9.4 0.0 copy-start.2
  9.4 88.6 %project_and_apply.1 = (f32[8,8,32,384]{3,2,1,0:T(8,128)S(1)}, f32[8,8,32,384]{3,2,1,0:T(8,128)S(1)}, f32[8,128]{1,0:T(8,128)S(1)}, f32[8,128]{1,0:T(8,128)S(1)}) custom-call(f32[8,8,32,384]{3,2,1,0:T(8,128)S(1)} %copy-done, f32[8,8,32,384]{3,2,1,0:T(8,128)S(1)} %copy-done.1, bf16[8,8,32,384]{3,2,1,0:T(8,128)(2,1)S(1)} %copy-done.3, ...), custom_call_target="tpu_custom_call" | custom-call | tf_op jit(solution)/shard_map/project_and_apply/pallas_call | solution.py:358
  98.1 0.6 slice_reduce_fusion
  98.7 0.0 copy-done.2
  98.7 4.9 %take_step.1 = (f32[8,8,32,384]{3,2,1,0:T(8,128)}, f32[8,8,32,384]{3,2,1,0:T(8,128)}, f32[8,8,32,384]{3,2,1,0:T(8,128)}) custom-call(f32[8,128]{1,0:T(8,128)S(1)} %get-tuple-element.11.step, f32[8,8,32,384]{3,2,1,0:T(8,128)S(1)} %copy-done.2, f32[8,8,32,384]{3,2,1,0:T(8,128)S(1)} %copy-done, f32[8,8,32,384]{3,2,1,0:T(8,128)S(1)} %get-tuple-element.12.new_dir, ...), custom_call_target="tpu_custom_call" | custom-call | tf_op jit(solution)/shard_map/take_step/pallas_call | solution.py:399
Async XLA Ops:
  0.6 1.9 %copy-start = (f32[8,8,32,384]{3,2,1,0:T(8,128)S(1)}, f32[8,8,32,384]{3,2,1,0:T(8,128)}, u32[]{:S(2)}) copy-start(f32[8,8,32,384]{3,2,1,0:T(8,128)} %residual_in.1) | copy-start | bytes 9437188
  2.5 1.9 %copy-start.1 = (f32[8,8,32,384]{3,2,1,0:T(8,128)S(1)}, f32[8,8,32,384]{3,2,1,0:T(8,128)}, u32[]{:S(2)}) copy-start(f32[8,8,32,384]{3,2,1,0:T(8,128)} %dir_hbm.1) | copy-start | bytes 9437188
  4.4 1.4 %copy-start.3 = (bf16[8,8,32,384]{3,2,1,0:T(8,128)(2,1)S(1)}, bf16[8,8,32,384]{3,2,1,0:T(8,128)(2,1)}, u32[]{:S(2)}) copy-start(bf16[8,8,32,384]{3,2,1,0:T(8,128)(2,1)} %orb_hbm.1) | copy-start | bytes 4718596
  5.8 1.0 copy-start.4
  6.8 0.7 copy-start.5
  7.5 0.7 copy-start.6
  8.1 0.7 copy-start.7
  8.8 0.7 copy-start.8
  9.4 89.2 %copy-start.2 = (f32[8,8,32,384]{3,2,1,0:T(8,128)S(1)}, f32[8,8,32,384]{3,2,1,0:T(8,128)}, u32[]{:S(2)}) copy-start(f32[8,8,32,384]{3,2,1,0:T(8,128)} %solution_in.1) | copy-start | bytes 9437188

commit v2 on v1

v2 whole, which is shorter than its diff:
```python
import functools

import jax
import jax.numpy as jnp
from jax import lax
from jax.experimental import pallas as pl
from jax.experimental.pallas import tpu as pltpu
from jax.sharding import PartitionSpec as P

MESH = pl.DeviceIdType.MESH
F32 = jnp.float32
BF16 = jnp.bfloat16

PB = 16
K0, K1, K2, K3 = (-49.0 / 18.0, 3.0 / 2.0, -3.0 / 20.0, 1.0 / 90.0)
SCALED = (135.0, -13.5, 1.0)
UNSCALE = -0.5 / 90.0

COLS = 8
BANDS = 8
XS = 8
NY = 32
NZ = 384
HALF = 16
HALO = 3
PIECES = (pl.ds(0, HALO), pl.ds(XS - HALO, HALO), pl.ds(HALO, XS - 2 * HALO))
FACES = PIECES[:2]


def iota(shape, dim):
    return lax.broadcasted_iota(jnp.int32, shape, dim)


def coefficient(distance):
    gap = jnp.abs(distance)
    return jnp.where(
        gap == 1, SCALED[0], jnp.where(gap == 2, SCALED[1], jnp.where(gap == 3, SCALED[2], 0.0))
    )


def dot(left, right, dims=((1,), (0,)), precision=None):
    return lax.dot_general(
        left, right, (dims, ((), ())), precision=precision, preferred_element_type=F32
    )


def first_kernel(
    groups,
    res_hbm,
    dir_hbm,
    orb_hbm,
    pot_hbm,
    old_hbm,
    energy_hbm,
    column_hbm,
    panel_hbm,
    new_dir,
    image,
    rr_out,
    step_out,
    start,
    direction,
    pot,
    wave,
    left,
    acc,
    kron,
    sten,
    sten_z,
    halo_wave,
    halo_out,
    halo_start,
    halo_in,
    halo_dir,
    sums,
    curves,
    partial,
    old_ref,
    energy_ref,
    column_ref,
    panel_ref,
    local_sem,
    ring_send,
    ring_recv,
    sum_send,
    sum_recv,
    halo_send,
    halo_recv,
):
    g = lax.axis_index("grid")
    z = lax.axis_index("band")
    up, down = lax.rem(z + 1, 4), lax.rem(z + 3, 4)

    loads = [
        pltpu.make_async_copy(src, dst, local_sem.at[i])
        for i, (src, dst) in enumerate(
            (
                (column_hbm, column_ref),
                (energy_hbm, energy_ref),
                (pot_hbm, pot),
                (res_hbm, start),
                (orb_hbm, wave.at[0]),
                (dir_hbm, direction),
                (old_hbm, old_ref),
                (panel_hbm, panel_ref),
            )
        )
    ]
    for load in loads:
        load.start()

    barrier = pltpu.get_barrier_semaphore()
    for to in (up, down):
        pl.semaphore_signal(barrier, inc=1, device_id=(g, to), device_id_type=MESH)

    for k in range(1, groups):
        pl.semaphore_signal(
            barrier, inc=1, device_id=(lax.rem(g + k, groups), z), device_id_type=MESH
        )
    pl.semaphore_wait(barrier, groups + 1)

    def ring(src, dst, i, to):
        return pltpu.make_async_remote_copy(
            src_ref=src,
            dst_ref=dst,
            send_sem=ring_send.at[i],
            recv_sem=ring_recv.at[i],
            device_id=(g, to),
            device_id_type=MESH,
        )

    sides = (lax.rem(g + groups - 1, groups), lax.rem(g + 1, groups))

    def halo(src, dst, i, face):
        return pltpu.make_async_remote_copy(
            src_ref=src,
            dst_ref=dst,
            send_sem=halo_send.at[i],
            recv_sem=halo_recv.at[i],
            device_id=(sides[face], z),
            device_id_type=MESH,
        )

    landing = (pl.ds(HALO, HALO), pl.ds(0, HALO))
    halos = []

    def send_faces(slot, bands, src=None):
        src = wave.at[slot] if src is None else src
        for face in range(2):
            send_face(slot, bands, face, src)

    def send_face(slot, bands, face, src):
        copy = halo(
            src.at[bands, FACES[face]], halo_wave.at[slot, bands, landing[face]], len(halos), face
        )
        copy.start()
        halos.append(copy)

    low, high = pl.ds(0, BANDS // 2), pl.ds(BANDS // 2, BANDS // 2)
    low_up = ring(orb_hbm.at[low], wave.at[1, low], 0, up)
    high_down = ring(orb_hbm.at[high], wave.at[3, high], 1, down)
    high_up = ring(orb_hbm.at[high], wave.at[1, high], 2, up)
    low_down = ring(orb_hbm.at[low], wave.at[3, low], 3, down)
    low_up.start()
    high_down.start()
    high_up.start()
    low_down.start()
    send_faces(0, pl.ds(0, BANDS), orb_hbm)

    rows, cols = iota((256, 448), 0), iota((256, 448), 1)
    plane = cols // NY
    there = jnp.where(plane < XS, plane, jnp.where(plane < XS + HALO, plane - XS - HALO, plane - HALO))
    inside = jnp.where(plane < XS, 1, jnp.where(plane < XS + HALO, g, groups - 1 - g)) > 0
    dx, dy = rows // NY - there, rows % NY - cols % NY
    weight = jnp.where(dy == 0, coefficient(dx), jnp.where(dx == 0, coefficient(dy), 0.0))
    sten[...] = jnp.where(inside, weight, 0.0).astype(BF16)
    sten_z[...] = coefficient(iota((NZ, NZ), 0) - iota((NZ, NZ), 1)).astype(BF16)

    def shift_of(c):
        return energy_ref[column_ref[c] // 3]

    for load in loads[:4]:
        load.wait()

    def start_column(c, _):
        e = shift_of(c)

        def start_plane(x, total):
            r = start[c, x]
            s = r / (pot[x] - e - 1.5 * K0)
            start[c, x] = s
            for h in range(2):
                part = slice(h * HALF, (h + 1) * HALF)
                left[x, h, 0, c] = s[part].astype(BF16)
                left[x, h, 1, c] = r[part].astype(BF16)
            return total + jnp.sum((r * s).reshape(4, 8, NZ), axis=0)

        total = lax.fori_loop(0, XS, start_plane, jnp.zeros((8, NZ), F32))
        partial[c] = total[:, :128] + total[:, 128:256] + total[:, 256:]
        return 0

    lax.fori_loop(0, COLS, start_column, 0)
    for face in range(2):
        copy = halo(start.at[:, FACES[face]], halo_start.at[:, landing[face]], len(halos), face)
        copy.start()
        halos.append(copy)
    loads[5].wait()

    def fill(c, _):
        for face in range(2):
            halo_out[face, c] = direction[c, FACES[face]].astype(BF16)
        return 0

    lax.fori_loop(0, COLS, fill, 0)
    for face in range(2):
        copy = halo(halo_out.at[face], halo_in.at[:, landing[face]], len(halos), face)
        copy.start()
        halos.append(copy)

    def correlate(slot, first, planes):
        def body(x, total):
            for h in range(2):
                total = total + dot(
                    left[x, h].reshape(256, NZ),
                    wave[slot, :, x, pl.ds(h * HALF, HALF), :].reshape(128, NZ),
                    ((1,), (1,)),
                )
            return total

        return lax.fori_loop(
            first, first + planes, body, jnp.zeros((256, 128), F32), unroll=planes <= HALO
        )

    loads[4].wait()
    acc[:, 0:128] = correlate(0, 0, XS)

    forwards = []
    low_up.wait_recv()
    for q, part in enumerate(PIECES):
        copy = ring(wave.at[1, low, part], wave.at[2, low, part], 4 + 2 * q, up)
        copy.start()
        forwards.append(copy)
    high_down.wait_recv()
    for q, part in enumerate(PIECES):
        copy = ring(wave.at[3, high, part], wave.at[2, high, part], 5 + 2 * q, down)
        copy.start()
        forwards.append(copy)
    send_faces(1, low)
    send_faces(3, high)
    high_up.wait_recv()
    send_faces(1, high)
    low_down.wait_recv()
    send_faces(3, low)
    acc[:, 128:256] = correlate(1, 0, XS)
    acc[:, 384:512] = correlate(3, 0, XS)
    for q, part in enumerate(PIECES):
        forwards[q].wait_recv()
        forwards[len(PIECES) + q].wait_recv()
        if q < 2:
            send_face(2, pl.ds(0, BANDS), q, wave.at[2])
        term = correlate(2, part.start, part.size)
        acc[:, 256:384] = term if q == 0 else acc[:, 256:384] + term

    same = iota((256, 512), 0) % HALF == iota((256, 512), 1) % HALF
    folded = jnp.sum(jnp.where(same, acc[...], 0.0).reshape(16, HALF, 512), axis=1)
    pick = iota((512, 128), 0) // HALF
    lane = iota((512, 128), 1)
    mine = dot(
        folded[:8], jnp.where(pick == lane, 1.0, 0.0), precision=lax.Precision.HIGHEST
    ) + dot(
        folded[8:], jnp.where(pick + 32 == lane, 1.0, 0.0), precision=lax.Precision.HIGHEST
    )
    lane = iota((8, 128), 1)
    own = jnp.sum(jnp.sum(partial[...], axis=1), axis=1, keepdims=True)
    mine = mine + jnp.where(lane == 64, own, 0.0)

    def add_over_grid(table, value, k):
        table[g] = value

        for i in range(1, groups):
            pltpu.make_async_remote_copy(
                src_ref=table.at[g],
                dst_ref=table.at[g],
                send_sem=sum_send.at[k],
                recv_sem=sum_recv.at[k],
                device_id=(lax.rem(g + i, groups), z),
                device_id_type=MESH,
            ).start()
        others = table.at[pl.ds(0, groups - 1)]
        pltpu.make_async_copy(others, others, sum_recv.at[k]).wait()
        total = jnp.sum(table[...], axis=0)
        pltpu.make_async_copy(others, others, sum_send.at[k]).wait()
        return total

    total = add_over_grid(sums, mine, 0)

    for load in loads[6:]:
        load.wait()
    owner = lax.rem(z + jnp.where(lane < 8, 0, jnp.where(lane < 16, 3, jnp.where(lane < 24, 2, 1))), 4)
    column = iota((8, 128), 0)
    panel = jnp.zeros((8, 128), jnp.int32)
    old = jnp.zeros((8, 128), F32)
    for c in range(COLS):
        panel = jnp.where(column == c, panel_ref[c], panel)
        old = jnp.where(column == c, old_ref[c], old)
    cells = float(groups * XS * NY * NZ)
    chosen = jnp.where(
        jnp.logical_and(lane < 32, owner * BANDS // PB == panel), total, 0.0
    ) / cells
    overlap = pltpu.roll(total, 96, 1)
    rr = jnp.sum(
        jnp.where(lane == 64, total, 0.0) - chosen * overlap, axis=1, keepdims=True
    )
    rr = jnp.broadcast_to(rr, (8, 128))
    rr_out[...] = rr
    beta = rr / old

    top = chosen.astype(BF16)
    rest = (chosen - top.astype(F32)).astype(BF16)
    pair = jnp.concatenate([top.astype(F32), rest.astype(F32)], axis=0).astype(BF16)
    spread = dot(
        jnp.where(iota((256, 16), 0) // HALF == iota((256, 16), 1), 1.0, 0.0).astype(BF16), pair
    ).astype(BF16)
    spread = dot(
        spread,
        jnp.where(iota((128, 512), 1) // HALF == iota((128, 512), 0), 1.0, 0.0).astype(BF16),
    )
    kron[...] = jnp.where(same, spread, 0.0).astype(BF16)

    def removed(source, x):
        plane = [
            source[:, :, x, h * HALF : (h + 1) * HALF, :].reshape(512, NZ) for h in range(2)
        ]
        both = dot(kron[...], jnp.concatenate(plane, axis=1))
        both = both[:128] + both[128:]
        return lambda c, h: both[c * HALF : (c + 1) * HALF, h * NZ : (h + 1) * NZ]

    for x in range(XS):
        gone = removed(wave, x)
        for c in range(COLS):
            for h in range(2):
                part = slice(h * HALF, (h + 1) * HALF)
                new_dir[c, x, part] = (
                    start[c, x, part] - gone(c, h) + beta[c : c + 1, :1] * direction[c, x, part]
                )
    for copy in halos:
        copy.wait_recv()
    for x in range(2 * HALO):
        gone = removed(halo_wave, x)
        for c in range(COLS):
            for h in range(2):
                part = slice(h * HALF, (h + 1) * HALF)
                halo_dir[c, x, part] = (
                    halo_start[c, x, part]
                    - gone(c, h)
                    + beta[c : c + 1, :1] * halo_in[c, x, part].astype(F32)
                ).astype(BF16)

    for c in range(COLS):
        value = new_dir[c].reshape(256, NZ)
        top = value.astype(BF16)
        beside = dot(
            sten[...], jnp.concatenate([top, halo_dir[c].reshape(192, NZ)], axis=0)
        ) + dot(top, sten_z[...])
        local = pot[...].reshape(256, NZ) - shift_of(c) - 1.5 * K0
        full = UNSCALE * beside + local * value
        image[c] = full.reshape(XS, NY, NZ)
        total = jnp.sum((full * value).reshape(32, 8, NZ), axis=0)
        partial[c] = total[:, :128] + total[:, 128:256] + total[:, 256:]
    curvature = jnp.sum(add_over_grid(curves, jnp.sum(partial[...], axis=1), 1), axis=1, keepdims=True)
    step_out[...] = rr / curvature

    for copy in (low_up, high_down, high_up, low_down, *forwards, *halos):
        copy.wait_send()


def last_kernel(
    step, rr, solution_in, residual_in, new_dir, image, solution_hbm, residual_hbm, dir_hbm, rr_out, solution_new, residual_new, sems
):
    copies = [pltpu.make_async_copy(new_dir, dir_hbm, sems.at[2 * COLS])]
    copies[0].start()
    lane, row = iota((8, 128), 1), iota((8, 128), 0)
    rr_out[...] = jnp.sum(jnp.where(lane == row, rr[...], 0.0), axis=0)[:COLS]
    for c in range(COLS):
        alpha = step[c : c + 1, :1]
        solution_new[c] = solution_in[c] + alpha * new_dir[c]
        residual_new[c] = residual_in[c] - alpha * image[c]
        for i, (src, dst) in enumerate(((solution_new, solution_hbm), (residual_new, residual_hbm))):
            copy = pltpu.make_async_copy(src.at[c], dst.at[c], sems.at[2 * c + i])
            copy.start()
            copies.append(copy)
    for copy in copies:
        copy.wait()


def on_device(groups, residual, direction, solution, old_product, orbitals, energies, potential, column_index, panel_index):
    field = (COLS, XS, NY, NZ)
    hbm = pl.BlockSpec(memory_space=pltpu.HBM)
    vmem = pl.BlockSpec(memory_space=pltpu.VMEM)
    dma = pltpu.SemaphoreType.DMA
    new_dir, image, rr, step = pl.pallas_call(
        functools.partial(first_kernel, groups),
        out_shape=(
            jax.ShapeDtypeStruct(field, F32),
            jax.ShapeDtypeStruct(field, F32),
            jax.ShapeDtypeStruct((8, 128), F32),
            jax.ShapeDtypeStruct((8, 128), F32),
        ),
        in_specs=[hbm] * 8,
        out_specs=(vmem, vmem, vmem, vmem),
        scratch_shapes=[
            pltpu.VMEM(field, F32),
            pltpu.VMEM(field, F32),
            pltpu.VMEM((XS, NY, NZ), F32),
            pltpu.VMEM((4, BANDS, XS, NY, NZ), BF16),
            pltpu.VMEM((XS, 2, 2, COLS, HALF, NZ), BF16),
            pltpu.VMEM((256, 512), F32),
            pltpu.VMEM((256, 512), BF16),
            pltpu.VMEM((256, 448), BF16),
            pltpu.VMEM((NZ, NZ), BF16),
            pltpu.VMEM((4, BANDS, 2 * HALO, NY, NZ), BF16),
            pltpu.VMEM((2, COLS, HALO, NY, NZ), BF16),
            pltpu.VMEM((COLS, 2 * HALO, NY, NZ), F32),
            pltpu.VMEM((COLS, 2 * HALO, NY, NZ), BF16),
            pltpu.VMEM((COLS, 2 * HALO, NY, NZ), BF16),
            pltpu.VMEM((groups, 8, 128), F32),
            pltpu.VMEM((groups, 8, 128), F32),
            pltpu.VMEM((COLS, 8, 128), F32),
            pltpu.SMEM((COLS,), F32),
            pltpu.SMEM((32,), F32),
            pltpu.SMEM((COLS,), jnp.int32),
            pltpu.SMEM((COLS,), jnp.int32),
            dma((8,)),
            dma((4 + 2 * len(PIECES),)),
            dma((4 + 2 * len(PIECES),)),
            dma((2,)),
            dma((2,)),
            dma((16,)),
            dma((16,)),
        ],
        compiler_params=pltpu.CompilerParams(
            collective_id=0, has_side_effects=True, vmem_limit_bytes=38 << 20
        ),
        name="project_and_apply",
    )(
        *(
            pltpu.with_memory_space_constraint(operand, pltpu.HBM)
            for operand in (
                residual,
                direction,
                orbitals,
                potential,
                old_product,
                energies,
                column_index,
                panel_index,
            )
        )
    )

    new_solution, new_residual, out_dir, new_product = pl.pallas_call(
        last_kernel,
        out_shape=(*(jax.ShapeDtypeStruct(field, F32) for _ in range(3)), jax.ShapeDtypeStruct((COLS,), F32)),
        in_specs=[vmem] * 6,
        out_specs=(hbm, hbm, hbm, vmem),
        scratch_shapes=[pltpu.VMEM(field, F32), pltpu.VMEM(field, F32), dma((2 * COLS + 1,))],
        compiler_params=pltpu.CompilerParams(vmem_limit_bytes=8 << 20),
        name="take_step",
    )(step, rr, solution, residual, new_dir, image)
    return new_solution, new_residual, out_dir, new_product


def solution(mesh):
    field = P("band", "grid", None, None)
    return jax.shard_map(
        functools.partial(on_device, mesh.shape["grid"]),
        mesh=mesh,
        in_specs=(
            field,
            field,
            field,
            P("band"),
            field,
            P(),
            P("grid", None, None),
            P("band"),
            P("band"),
        ),
        out_specs=(field, field, field, P("band")),
        check_vma=False,
    )
```

time: 104 us -> 86 us (0.83)
  local copies, waits for them, and re-layouts: 9.42 us -> 0.01 us
  Pallas kernels: 93.5 us -> 85.2 us
    unnamed x18 -> x4, local copies, waits for them, and re-layouts: 8.8 us -> 0.01 us
    pallas_call x1, Pallas kernels: 88.6 us -> 80.9 us  [on_device(): pl.pallas_call(functools.partial(first_kernel, groups), out_shape=(jax.Sh...]
where the time goes in v2:
time: 86 us; the launch traced here: 85.9 us
  Pallas kernels  85.2 us (99%)
    pallas_call x1, Pallas kernels, on_device(): pl.pallas_call(functools.partial(first_kernel, groups), out_shape=(jax.Sh...  80.9 us
    pallas_call x1, Pallas kernels, on_device(): pl.pallas_call(last_kernel, out_shape=(*(jax.ShapeDtypeStruct(field, F32)...  4.25 us

profile of v2, /device:TPU:1, one launch (start us, length us, event | category | flops | bytes accessed | tf_op | source)
XLA Modules:
  0.0 85.9 jit_solution(3439210935907358026)
XLA Ops:
  0.6 0.0 copy-start
  0.6 0.0 copy-start.1
  0.7 80.9 %project_and_apply.1 = (f32[8,8,32,384]{3,2,1,0:T(8,128)S(1)}, f32[8,8,32,384]{3,2,1,0:T(8,128)S(1)}, f32[8,128]{1,0:T(8,128)S(1)}, f32[8,128]{1,0:T(8,128)S(1)}) custom-call(f32[8,8,32,384]{3,2,1,0:T(8,128)} %residual_in.1, f32[8,8,32,384]{3,2,1,0:T(8,128)} %dir_hbm.1, bf16[8,8,32,384]{3,2,1,0:T(8,128)(2,1)} %orb_hbm.1, f32[8,32,384]{2,1,0:T(8,128)} %pot_hbm.1, ...), custom_call_target="tpu_custom_call" | custom-call | tf_op jit(solution)/shard_map/project_and_apply/pallas_call | solution.py:401
  81.6 0.0 copy-done
  81.6 0.0 copy-done.1
  81.6 4.2 %take_step.1 = (f32[8,8,32,384]{3,2,1,0:T(8,128)}, f32[8,8,32,384]{3,2,1,0:T(8,128)}, f32[8,8,32,384]{3,2,1,0:T(8,128)}, f32[8]{0:T(128)}) custom-call(f32[8,128]{1,0:T(8,128)S(1)} %get-tuple-element.8.step, f32[8,128]{1,0:T(8,128)S(1)} %get-tuple-element.9.rr, f32[8,8,32,384]{3,2,1,0:T(8,128)S(1)} %copy-done.1, f32[8,8,32,384]{3,2,1,0:T(8,128)S(1)} %copy-done, ...), custom_call_target="tpu_custom_call" | custom-call | tf_op jit(solution)/shard_map/take_step/pallas_call | solution.py:461
Async XLA Ops:
  0.6 81.0 %copy-start = (f32[8,8,32,384]{3,2,1,0:T(8,128)S(1)}, f32[8,8,32,384]{3,2,1,0:T(8,128)}, u32[]{:S(2)}) copy-start(f32[8,8,32,384]{3,2,1,0:T(8,128)} %residual_in.1) | copy-start | bytes 9437188
  0.6 81.0 %copy-start.1 = (f32[8,8,32,384]{3,2,1,0:T(8,128)S(1)}, f32[8,8,32,384]{3,2,1,0:T(8,128)}, u32[]{:S(2)}) copy-start(f32[8,8,32,384]{3,2,1,0:T(8,128)} %solution_in.1) | copy-start | bytes 9437188

commit v3 on v2

--- a/solution.py
+++ b/solution.py
@@ -23,8 +23,9 @@
 NZ = 384
 HALF = 16
 HALO = 3
-PIECES = (pl.ds(0, HALO), pl.ds(XS - HALO, HALO), pl.ds(HALO, XS - 2 * HALO))
-FACES = PIECES[:2]
+FACES = (pl.ds(0, HALO), pl.ds(XS - HALO, HALO))
+PIECES = (pl.ds(0, 2), pl.ds(XS - 2, 2), pl.ds(2, 1), pl.ds(XS - 3, 1), pl.ds(HALO, XS - 2 * HALO))
+TURNS = 4
 
 
 def iota(shape, dim):
@@ -63,7 +64,6 @@
     pot,
     wave,
     left,
-    acc,
     kron,
     sten,
     sten_z,
@@ -106,9 +106,6 @@
             )
         )
     ]
-    for load in loads:
-        load.start()
-
     barrier = pltpu.get_barrier_semaphore()
     for to in (up, down):
         pl.semaphore_signal(barrier, inc=1, device_id=(g, to), device_id_type=MESH)
@@ -117,6 +114,8 @@
         pl.semaphore_signal(
             barrier, inc=1, device_id=(lax.rem(g + k, groups), z), device_id_type=MESH
         )
+    for load in loads:
+        load.start()
     pl.semaphore_wait(barrier, groups + 1)
 
     def ring(src, dst, i, to):
@@ -147,12 +146,10 @@
     def send_faces(slot, bands, src=None):
         src = wave.at[slot] if src is None else src
         for face in range(2):
-            send_face(slot, bands, face, src)
-
-    def send_face(slot, bands, face, src):
-        copy = halo(
-            src.at[bands, FACES[face]], halo_wave.at[slot, bands, landing[face]], len(halos), face
-        )
+            send_face(slot, bands, face, src, FACES[face], landing[face])
+
+    def send_face(slot, bands, face, src, planes, place):
+        copy = halo(src.at[bands, planes], halo_wave.at[slot, bands, place], len(halos), face)
         copy.start()
         halos.append(copy)
 
@@ -231,8 +228,23 @@
             first, first + planes, body, jnp.zeros((256, 128), F32), unroll=planes <= HALO
         )
 
+    lane = iota((8, 128), 1)
+    own = jnp.sum(jnp.sum(partial[...], axis=1), axis=1, keepdims=True)
+    same = iota((256, 128), 0) % HALF == iota((256, 128), 1) % HALF
+
+    def fold(block, slot):
+        rows = jnp.sum(jnp.where(same, block, 0.0).reshape(16, HALF, 128), axis=1)
+        high = rows.astype(BF16).astype(F32)
+        middle = (rows - high).astype(BF16).astype(F32)
+        terms = jnp.concatenate([high, middle, rows - high - middle], axis=0).astype(BF16)
+        pick = iota((128, 128), 0) // HALF + slot * BANDS
+        ones = jnp.where(pick == iota((128, 128), 1), 1.0, 0.0).astype(BF16)
+        parts = dot(terms, ones)
+        parts = parts[:16] + parts[16:32] + parts[32:]
+        return parts[:8] + pltpu.roll(parts[8:], 32, 1)
+
     loads[4].wait()
-    acc[:, 0:128] = correlate(0, 0, XS)
+    mine = fold(correlate(0, 0, XS), 0)
 
     forwards = []
     low_up.wait_recv()
@@ -251,33 +263,29 @@
     send_faces(1, high)
     low_down.wait_recv()
     send_faces(3, low)
-    acc[:, 128:256] = correlate(1, 0, XS)
-    acc[:, 384:512] = correlate(3, 0, XS)
+    mine = mine + fold(correlate(1, 0, XS), 1)
+    mine = mine + fold(correlate(3, 0, XS), 3)
+    mine = mine + jnp.where(lane == 64, own, 0.0)
     for q, part in enumerate(PIECES):
         forwards[q].wait_recv()
         forwards[len(PIECES) + q].wait_recv()
-        if q < 2:
-            send_face(2, pl.ds(0, BANDS), q, wave.at[2])
+        if q < TURNS:
+            place = pl.ds(part.start + (HALO if q % 2 == 0 else HALO - XS), part.size)
+            send_face(2, pl.ds(0, BANDS), q % 2, wave.at[2], part, place)
         term = correlate(2, part.start, part.size)
-        acc[:, 256:384] = term if q == 0 else acc[:, 256:384] + term
-
-    same = iota((256, 512), 0) % HALF == iota((256, 512), 1) % HALF
-    folded = jnp.sum(jnp.where(same, acc[...], 0.0).reshape(16, HALF, 512), axis=1)
-    pick = iota((512, 128), 0) // HALF
-    lane = iota((512, 128), 1)
-    mine = dot(
-        folded[:8], jnp.where(pick == lane, 1.0, 0.0), precision=lax.Precision.HIGHEST
-    ) + dot(
-        folded[8:], jnp.where(pick + 32 == lane, 1.0, 0.0), precision=lax.Precision.HIGHEST
-    )
-    lane = iota((8, 128), 1)
-    own = jnp.sum(jnp.sum(partial[...], axis=1), axis=1, keepdims=True)
-    mine = mine + jnp.where(lane == 64, own, 0.0)
+        last = term if q == 0 else last + term
+    mine = mine + fold(last, 2)
+
+    def far(i):
+        steps = (i // 8, i // 2 % 4)
+        return -sum(min(n, 4 - n) for n in steps)
+
+    order = sorted(range(1, groups), key=far)
 
     def add_over_grid(table, value, k):
         table[g] = value
 
-        for i in range(1, groups):
+        for i in order:
             pltpu.make_async_remote_copy(
                 src_ref=table.at[g],
                 dst_ref=table.at[g],
@@ -288,9 +296,7 @@
             ).start()
         others = table.at[pl.ds(0, groups - 1)]
         pltpu.make_async_copy(others, others, sum_recv.at[k]).wait()
-        total = jnp.sum(table[...], axis=0)
-        pltpu.make_async_copy(others, others, sum_send.at[k]).wait()
-        return total
+        return jnp.sum(table[...], axis=0)
 
     total = add_over_grid(sums, mine, 0)
 
@@ -319,12 +325,11 @@
     rest = (chosen - top.astype(F32)).astype(BF16)
     pair = jnp.concatenate([top.astype(F32), rest.astype(F32)], axis=0).astype(BF16)
     spread = dot(
-        jnp.where(iota((256, 16), 0) // HALF == iota((256, 16), 1), 1.0, 0.0).astype(BF16), pair
-    ).astype(BF16)
-    spread = dot(
-        spread,
+        pair,
         jnp.where(iota((128, 512), 1) // HALF == iota((128, 512), 0), 1.0, 0.0).astype(BF16),
     )
+    spread = jnp.broadcast_to(spread[:, None, :], (16, HALF, 512)).reshape(256, 512)
+    same = iota((256, 512), 0) % HALF == iota((256, 512), 1) % HALF
     kron[...] = jnp.where(same, spread, 0.0).astype(BF16)
 
     def removed(source, x):
@@ -370,6 +375,9 @@
     curvature = jnp.sum(add_over_grid(curves, jnp.sum(partial[...], axis=1), 1), axis=1, keepdims=True)
     step_out[...] = rr / curvature
 
+    for k, table in enumerate((sums, curves)):
+        others = table.at[pl.ds(0, groups - 1)]
+        pltpu.make_async_copy(others, others, sum_send.at[k]).wait()
     for copy in (low_up, high_down, high_up, low_down, *forwards, *halos):
         copy.wait_send()
 
@@ -414,7 +422,6 @@
             pltpu.VMEM((XS, NY, NZ), F32),
             pltpu.VMEM((4, BANDS, XS, NY, NZ), BF16),
             pltpu.VMEM((XS, 2, 2, COLS, HALF, NZ), BF16),
-            pltpu.VMEM((256, 512), F32),
             pltpu.VMEM((256, 512), BF16),
             pltpu.VMEM((256, 448), BF16),
             pltpu.VMEM((NZ, NZ), BF16),
@@ -435,8 +442,8 @@
             dma((4 + 2 * len(PIECES),)),
             dma((2,)),
             dma((2,)),
-            dma((16,)),
-            dma((16,)),
+            dma((14 + TURNS,)),
+            dma((14 + TURNS,)),
         ],
         compiler_params=pltpu.CompilerParams(
             collective_id=0, has_side_effects=True, vmem_limit_bytes=38 << 20

time: 86 us -> 84.7 us (0.985)
  Pallas kernels: 85.2 us -> 83.9 us
    pallas_call x1, Pallas kernels: 80.9 us -> 79.6 us  [on_device(): pl.pallas_call(functools.partial(first_kernel, groups), out_shape=(jax.Sh...]
where the time goes in v3:
time: 84.7 us; the launch traced here: 84.6 us
  Pallas kernels  83.9 us (99%)
    pallas_call x1, Pallas kernels, on_device(): pl.pallas_call(functools.partial(first_kernel, groups), out_shape=(jax.Sh...  79.6 us
    pallas_call x1, Pallas kernels, on_device(): pl.pallas_call(last_kernel, out_shape=(*(jax.ShapeDtypeStruct(field, F32)...  4.25 us

profile of v3, /device:TPU:1, one launch (start us, length us, event | category | flops | bytes accessed | tf_op | source)
XLA Modules:
  0.0 84.6 jit_solution(9136846080041465590)
XLA Ops:
  0.6 0.0 copy-start
  0.6 0.0 copy-start.1
  0.7 79.6 %project_and_apply.1 = (f32[8,8,32,384]{3,2,1,0:T(8,128)S(1)}, f32[8,8,32,384]{3,2,1,0:T(8,128)S(1)}, f32[8,128]{1,0:T(8,128)S(1)}, f32[8,128]{1,0:T(8,128)S(1)}) custom-call(f32[8,8,32,384]{3,2,1,0:T(8,128)} %residual_in.1, f32[8,8,32,384]{3,2,1,0:T(8,128)} %dir_hbm.1, bf16[8,8,32,384]{3,2,1,0:T(8,128)(2,1)} %orb_hbm.1, f32[8,32,384]{2,1,0:T(8,128)} %pot_hbm.1, ...), custom_call_target="tpu_custom_call" | custom-call | tf_op jit(solution)/shard_map/project_and_apply/pallas_call | solution.py:409
  80.3 0.0 copy-done
  80.3 0.0 copy-done.1
  80.3 4.2 %take_step.1 = (f32[8,8,32,384]{3,2,1,0:T(8,128)}, f32[8,8,32,384]{3,2,1,0:T(8,128)}, f32[8,8,32,384]{3,2,1,0:T(8,128)}, f32[8]{0:T(128)}) custom-call(f32[8,128]{1,0:T(8,128)S(1)} %get-tuple-element.8.step, f32[8,128]{1,0:T(8,128)S(1)} %get-tuple-element.9.rr, f32[8,8,32,384]{3,2,1,0:T(8,128)S(1)} %copy-done.1, f32[8,8,32,384]{3,2,1,0:T(8,128)S(1)} %copy-done, ...), custom_call_target="tpu_custom_call" | custom-call | tf_op jit(solution)/shard_map/take_step/pallas_call | solution.py:468
Async XLA Ops:
  0.6 79.7 %copy-start = (f32[8,8,32,384]{3,2,1,0:T(8,128)S(1)}, f32[8,8,32,384]{3,2,1,0:T(8,128)}, u32[]{:S(2)}) copy-start(f32[8,8,32,384]{3,2,1,0:T(8,128)} %residual_in.1) | copy-start | bytes 9437188
  0.6 79.7 %copy-start.1 = (f32[8,8,32,384]{3,2,1,0:T(8,128)S(1)}, f32[8,8,32,384]{3,2,1,0:T(8,128)}, u32[]{:S(2)}) copy-start(f32[8,8,32,384]{3,2,1,0:T(8,128)} %solution_in.1) | copy-start | bytes 9437188

commit v4 on v3

--- a/solution.py
+++ b/solution.py
@@ -55,16 +55,21 @@
     energy_hbm,
     column_hbm,
     panel_hbm,
+    solution_hbm,
     new_dir,
     image,
     rr_out,
     step_out,
+    residual_near,
+    solution_near,
     start,
     direction,
     pot,
     wave,
     left,
     kron,
+    kron_mask,
+    kron_ones,
     sten,
     sten_z,
     halo_wave,
@@ -103,6 +108,8 @@
                 (dir_hbm, direction),
                 (old_hbm, old_ref),
                 (panel_hbm, panel_ref),
+                (res_hbm, residual_near),
+                (solution_hbm, solution_near),
             )
         )
     ]
@@ -114,8 +121,6 @@
         pl.semaphore_signal(
             barrier, inc=1, device_id=(lax.rem(g + k, groups), z), device_id_type=MESH
         )
-    for load in loads:
-        load.start()
     pl.semaphore_wait(barrier, groups + 1)
 
     def ring(src, dst, i, to):
@@ -162,8 +167,8 @@
     high_down.start()
     high_up.start()
     low_down.start()
-    send_faces(0, pl.ds(0, BANDS), orb_hbm)
-
+    for load in loads[:5]:
+        load.start()
     rows, cols = iota((256, 448), 0), iota((256, 448), 1)
     plane = cols // NY
     there = jnp.where(plane < XS, plane, jnp.where(plane < XS + HALO, plane - XS - HALO, plane - HALO))
@@ -196,7 +201,10 @@
         partial[c] = total[:, :128] + total[:, 128:256] + total[:, 256:]
         return 0
 
+    for load in loads[5:]:
+        load.start()
     lax.fori_loop(0, COLS, start_column, 0)
+    send_faces(0, pl.ds(0, BANDS), orb_hbm)
     for face in range(2):
         copy = halo(start.at[:, FACES[face]], halo_start.at[:, landing[face]], len(halos), face)
         copy.start()
@@ -282,7 +290,7 @@
 
     order = sorted(range(1, groups), key=far)
 
-    def add_over_grid(table, value, k):
+    def send_over_grid(table, value, k):
         table[g] = value
 
         for i in order:
@@ -294,11 +302,12 @@
                 device_id=(lax.rem(g + i, groups), z),
                 device_id_type=MESH,
             ).start()
+    def sum_over_grid(table, k):
         others = table.at[pl.ds(0, groups - 1)]
         pltpu.make_async_copy(others, others, sum_recv.at[k]).wait()
         return jnp.sum(table[...], axis=0)
 
-    total = add_over_grid(sums, mine, 0)
+    send_over_grid(sums, mine, 0)
 
     for load in loads[6:]:
         load.wait()
@@ -309,10 +318,17 @@
     for c in range(COLS):
         panel = jnp.where(column == c, panel_ref[c], panel)
         old = jnp.where(column == c, old_ref[c], old)
+    mask = jnp.where(iota((256, 512), 0) % HALF == iota((256, 512), 1) % HALF, 1.0, 0.0)
+    kron_mask[...] = mask.astype(BF16)
+    widen = jnp.where(iota((128, 512), 1) // HALF == iota((128, 512), 0), 1.0, 0.0)
+    kron_ones[...] = widen.astype(BF16)
+    member = jnp.logical_and(lane < 32, owner * BANDS // PB == panel)
+    for copy in halos:
+        copy.wait_recv()
+    total = sum_over_grid(sums, 0)
+
     cells = float(groups * XS * NY * NZ)
-    chosen = jnp.where(
-        jnp.logical_and(lane < 32, owner * BANDS // PB == panel), total, 0.0
-    ) / cells
+    chosen = jnp.where(member, total, 0.0) / cells
     overlap = pltpu.roll(total, 96, 1)
     rr = jnp.sum(
         jnp.where(lane == 64, total, 0.0) - chosen * overlap, axis=1, keepdims=True
@@ -324,13 +340,9 @@
     top = chosen.astype(BF16)
     rest = (chosen - top.astype(F32)).astype(BF16)
     pair = jnp.concatenate([top.astype(F32), rest.astype(F32)], axis=0).astype(BF16)
-    spread = dot(
-        pair,
-        jnp.where(iota((128, 512), 1) // HALF == iota((128, 512), 0), 1.0, 0.0).astype(BF16),
-    )
+    spread = dot(pair, kron_ones[...])
     spread = jnp.broadcast_to(spread[:, None, :], (16, HALF, 512)).reshape(256, 512)
-    same = iota((256, 512), 0) % HALF == iota((256, 512), 1) % HALF
-    kron[...] = jnp.where(same, spread, 0.0).astype(BF16)
+    kron[...] = spread.astype(BF16) * kron_mask[...]
 
     def removed(source, x):
         plane = [
@@ -348,8 +360,6 @@
                 new_dir[c, x, part] = (
                     start[c, x, part] - gone(c, h) + beta[c : c + 1, :1] * direction[c, x, part]
                 )
-    for copy in halos:
-        copy.wait_recv()
     for x in range(2 * HALO):
         gone = removed(halo_wave, x)
         for c in range(COLS):
@@ -361,25 +371,38 @@
                     + beta[c : c + 1, :1] * halo_in[c, x, part].astype(F32)
                 ).astype(BF16)
 
-    for c in range(COLS):
-        value = new_dir[c].reshape(256, NZ)
-        top = value.astype(BF16)
-        beside = dot(
-            sten[...], jnp.concatenate([top, halo_dir[c].reshape(192, NZ)], axis=0)
-        ) + dot(top, sten_z[...])
-        local = pot[...].reshape(256, NZ) - shift_of(c) - 1.5 * K0
-        full = UNSCALE * beside + local * value
-        image[c] = full.reshape(XS, NY, NZ)
-        total = jnp.sum((full * value).reshape(32, 8, NZ), axis=0)
-        partial[c] = total[:, :128] + total[:, 128:256] + total[:, 256:]
-    curvature = jnp.sum(add_over_grid(curves, jnp.sum(partial[...], axis=1), 1), axis=1, keepdims=True)
-    step_out[...] = rr / curvature
-
-    for k, table in enumerate((sums, curves)):
+    for first in range(0, COLS, 2):
+        pair = [new_dir[c].reshape(256, NZ) for c in (first, first + 1)]
+        tops = [value.astype(BF16) for value in pair]
+        around = [
+            jnp.concatenate([top, halo_dir[first + i].reshape(192, NZ)], axis=0)
+            for i, top in enumerate(tops)
+        ]
+        across = dot(sten[...], jnp.concatenate(around, axis=1))
+        for i, (value, top) in enumerate(zip(pair, tops)):
+            c = first + i
+            along = [
+                dot(top, sten_z[:, 0:256]),
+                dot(top[:, 128:384], sten_z[128:384, 256:384]),
+            ]
+            beside = across[:, i * NZ : (i + 1) * NZ] + jnp.concatenate(along, axis=1)
+            local = pot[...].reshape(256, NZ) - (shift_of(c) + 1.5 * K0)
+            full = UNSCALE * beside + local * value
+            image[c] = full.reshape(XS, NY, NZ)
+            total = jnp.sum((full * value).reshape(32, 8, NZ), axis=0)
+            partial[c] = total[:, :128] + total[:, 128:256] + total[:, 256:]
+    send_over_grid(curves, jnp.sum(partial[...], axis=1), 1)
+
+    def drain(table, k):
         others = table.at[pl.ds(0, groups - 1)]
         pltpu.make_async_copy(others, others, sum_send.at[k]).wait()
+
+    drain(sums, 0)
     for copy in (low_up, high_down, high_up, low_down, *forwards, *halos):
         copy.wait_send()
+    drain(curves, 1)
+    curvature = jnp.sum(sum_over_grid(curves, 1), axis=1, keepdims=True)
+    step_out[...] = rr / curvature
 
 
 def last_kernel(
@@ -406,16 +429,18 @@
     hbm = pl.BlockSpec(memory_space=pltpu.HBM)
     vmem = pl.BlockSpec(memory_space=pltpu.VMEM)
     dma = pltpu.SemaphoreType.DMA
-    new_dir, image, rr, step = pl.pallas_call(
+    new_dir, image, rr, step, residual, solution = pl.pallas_call(
         functools.partial(first_kernel, groups),
         out_shape=(
             jax.ShapeDtypeStruct(field, F32),
             jax.ShapeDtypeStruct(field, F32),
             jax.ShapeDtypeStruct((8, 128), F32),
             jax.ShapeDtypeStruct((8, 128), F32),
+            jax.ShapeDtypeStruct(field, F32),
+            jax.ShapeDtypeStruct(field, F32),
         ),
-        in_specs=[hbm] * 8,
-        out_specs=(vmem, vmem, vmem, vmem),
+        in_specs=[hbm] * 9,
+        out_specs=(vmem,) * 6,
         scratch_shapes=[
             pltpu.VMEM(field, F32),
             pltpu.VMEM(field, F32),
@@ -423,6 +448,8 @@
             pltpu.VMEM((4, BANDS, XS, NY, NZ), BF16),
             pltpu.VMEM((XS, 2, 2, COLS, HALF, NZ), BF16),
             pltpu.VMEM((256, 512), BF16),
+            pltpu.VMEM((256, 512), BF16),
+            pltpu.VMEM((128, 512), BF16),
             pltpu.VMEM((256, 448), BF16),
             pltpu.VMEM((NZ, NZ), BF16),
             pltpu.VMEM((4, BANDS, 2 * HALO, NY, NZ), BF16),
@@ -437,7 +464,7 @@
             pltpu.SMEM((32,), F32),
             pltpu.SMEM((COLS,), jnp.int32),
             pltpu.SMEM((COLS,), jnp.int32),
-            dma((8,)),
+            dma((10,)),
             dma((4 + 2 * len(PIECES),)),
             dma((4 + 2 * len(PIECES),)),
             dma((2,)),
@@ -461,6 +488,7 @@
                 energies,
                 column_index,
                 panel_index,
+                solution,
             )
         )
     )

time: 84.7 us -> 84 us (level)
  no operation moved by 1% of the time
where the time goes in v4:
time: 84 us; the launch traced here: 83.9 us
  Pallas kernels  83.3 us (99%)
    pallas_call x1, Pallas kernels, on_device(): pl.pallas_call(functools.partial(first_kernel, groups), out_shape=(jax.Sh...  79 us
    pallas_call x1, Pallas kernels, on_device(): pl.pallas_call(last_kernel, out_shape=(*(jax.ShapeDtypeStruct(field, F32)...  4.25 us

profile of v4, /device:TPU:1, one launch (start us, length us, event | category | flops | bytes accessed | tf_op | source)
XLA Modules:
  0.0 83.9 jit_solution(4551199017001527936)
XLA Ops:
  0.6 79.0 %project_and_apply.1 = (f32[8,8,32,384]{3,2,1,0:T(8,128)S(1)}, f32[8,8,32,384]{3,2,1,0:T(8,128)S(1)}, f32[8,128]{1,0:T(8,128)S(1)}, f32[8,128]{1,0:T(8,128)S(1)}...) custom-call(f32[8,8,32,384]{3,2,1,0:T(8,128)} %res_hbm.1, f32[8,8,32,384]{3,2,1,0:T(8,128)} %dir_hbm.1, ...), custom_call_target="tpu_custom_call" | custom-call | tf_op jit(solution)/shard_map/project_and_apply/pallas_call | solution.py:432
  79.7 4.2 %take_step.1 = (f32[8,8,32,384]{3,2,1,0:T(8,128)}, f32[8,8,32,384]{3,2,1,0:T(8,128)}, f32[8,8,32,384]{3,2,1,0:T(8,128)}, f32[8]{0:T(128)}) custom-call(f32[8,128]{1,0:T(8,128)S(1)} %get-tuple-element.10.step, f32[8,128]{1,0:T(8,128)S(1)} %get-tuple-element.11.rr, f32[8,8,32,384]{3,2,1,0:T(8,128)S(1)} %get-tuple-element.12.solution_in, ...), custom_call_target="tpu_custom_call" | custom-call | tf_op jit(solution)/shard_map/take_step/pallas_call | solution.py:496

commit v5 on v4

--- a/solution.py
+++ b/solution.py
@@ -113,11 +113,17 @@
             )
         )
     ]
+    def far(i):
+        steps = (i // 8, i // 2 % 4)
+        return -sum(min(n, 4 - n) for n in steps)
+
+    order = sorted(range(1, groups), key=far)
+
     barrier = pltpu.get_barrier_semaphore()
     for to in (up, down):
         pl.semaphore_signal(barrier, inc=1, device_id=(g, to), device_id_type=MESH)
 
-    for k in range(1, groups):
+    for k in order:
         pl.semaphore_signal(
             barrier, inc=1, device_id=(lax.rem(g + k, groups), z), device_id_type=MESH
         )
@@ -284,28 +290,23 @@
         last = term if q == 0 else last + term
     mine = mine + fold(last, 2)
 
-    def far(i):
-        steps = (i // 8, i // 2 % 4)
-        return -sum(min(n, 4 - n) for n in steps)
-
-    order = sorted(range(1, groups), key=far)
-
     def send_over_grid(table, value, k):
-        table[g] = value
+        rows = pl.ds(0, value.shape[0])
+        table[g, rows] = value
 
         for i in order:
             pltpu.make_async_remote_copy(
-                src_ref=table.at[g],
-                dst_ref=table.at[g],
+                src_ref=table.at[g, rows],
+                dst_ref=table.at[g, rows],
                 send_sem=sum_send.at[k],
                 recv_sem=sum_recv.at[k],
                 device_id=(lax.rem(g + i, groups), z),
                 device_id_type=MESH,
             ).start()
-    def sum_over_grid(table, k):
-        others = table.at[pl.ds(0, groups - 1)]
+    def sum_over_grid(table, k, count):
+        others = table.at[pl.ds(0, groups - 1), pl.ds(0, count)]
         pltpu.make_async_copy(others, others, sum_recv.at[k]).wait()
-        return jnp.sum(table[...], axis=0)
+        return jnp.sum(table[:, :count], axis=0)
 
     send_over_grid(sums, mine, 0)
 
@@ -325,7 +326,7 @@
     member = jnp.logical_and(lane < 32, owner * BANDS // PB == panel)
     for copy in halos:
         copy.wait_recv()
-    total = sum_over_grid(sums, 0)
+    total = sum_over_grid(sums, 0, 8)
 
     cells = float(groups * XS * NY * NZ)
     chosen = jnp.where(member, total, 0.0) / cells
@@ -391,17 +392,20 @@
             image[c] = full.reshape(XS, NY, NZ)
             total = jnp.sum((full * value).reshape(32, 8, NZ), axis=0)
             partial[c] = total[:, :128] + total[:, 128:256] + total[:, 256:]
-    send_over_grid(curves, jnp.sum(partial[...], axis=1), 1)
-
-    def drain(table, k):
-        others = table.at[pl.ds(0, groups - 1)]
+    diagonal = iota((8, 128), 0) == lane
+    curved = jnp.sum(jnp.sum(partial[...], axis=1), axis=1, keepdims=True)
+    send_over_grid(curves, jnp.sum(jnp.where(diagonal, curved, 0.0), axis=0, keepdims=True), 1)
+
+    def drain(table, k, count):
+        others = table.at[pl.ds(0, groups - 1), pl.ds(0, count)]
         pltpu.make_async_copy(others, others, sum_send.at[k]).wait()
 
-    drain(sums, 0)
+    drain(sums, 0, 8)
     for copy in (low_up, high_down, high_up, low_down, *forwards, *halos):
         copy.wait_send()
-    drain(curves, 1)
-    curvature = jnp.sum(sum_over_grid(curves, 1), axis=1, keepdims=True)
+    drain(curves, 1, 1)
+    curvature = jnp.where(diagonal, sum_over_grid(curves, 1, 1), 0.0)
+    curvature = jnp.sum(curvature, axis=1, keepdims=True)
     step_out[...] = rr / curvature
 
 

time: 84 us -> 83 us (0.988)
  Pallas kernels: 83.3 us -> 82.2 us
    pallas_call x1, Pallas kernels: 79 us -> 78 us  [on_device(): pl.pallas_call(functools.partial(first_kernel, groups), out_shape=(jax.Sh...]
where the time goes in v5:
time: 83 us; the launch traced here: 82.9 us
  Pallas kernels  82.2 us (99%)
    pallas_call x1, Pallas kernels, on_device(): pl.pallas_call(functools.partial(first_kernel, groups), out_shape=(jax.Sh...  78 us
    pallas_call x1, Pallas kernels, on_device(): pl.pallas_call(last_kernel, out_shape=(*(jax.ShapeDtypeStruct(field, F32)...  4.25 us

profile of v5, /device:TPU:1, one launch (start us, length us, event | category | flops | bytes accessed | tf_op | source)
XLA Modules:
  0.0 82.9 jit_solution(1028523744519548640)
XLA Ops:
  0.6 78.0 %project_and_apply.1 = (f32[8,8,32,384]{3,2,1,0:T(8,128)S(1)}, f32[8,8,32,384]{3,2,1,0:T(8,128)S(1)}, f32[8,128]{1,0:T(8,128)S(1)}, f32[8,128]{1,0:T(8,128)S(1)}...) custom-call(f32[8,8,32,384]{3,2,1,0:T(8,128)} %res_hbm.1, f32[8,8,32,384]{3,2,1,0:T(8,128)} %dir_hbm.1, ...), custom_call_target="tpu_custom_call" | custom-call | tf_op jit(solution)/shard_map/project_and_apply/pallas_call | solution.py:436
  78.6 4.2 %take_step.1 = (f32[8,8,32,384]{3,2,1,0:T(8,128)}, f32[8,8,32,384]{3,2,1,0:T(8,128)}, f32[8,8,32,384]{3,2,1,0:T(8,128)}, f32[8]{0:T(128)}) custom-call(f32[8,128]{1,0:T(8,128)S(1)} %get-tuple-element.10.step, f32[8,128]{1,0:T(8,128)S(1)} %get-tuple-element.11.rr, f32[8,8,32,384]{3,2,1,0:T(8,128)S(1)} %get-tuple-element.12.solution_in, ...), custom_call_target="tpu_custom_call" | custom-call | tf_op jit(solution)/shard_map/take_step/pallas_call | solution.py:500
